TPU v7x, 1024 devices: a whole 4x8x16 slice. The times are simulated.
1024 devices in a mesh: dp: 16 (over z_lo, x), expert: 64 (over y, z_hi, core).
Axes of the slice: x: 4, y: 8, z: 16 (z_hi: 4, z_lo: 4; z = z_hi * 4 + z_lo), core: 2. Of those that a mesh axis runs over, the one named last changes fastest.
Arguments:
- compressed_tokens: bfloat16 [262144, 512], P(('dp', 'expert')), may hold values from -6 to 6
- picked_specialists: int32 [262144, 8], P(('dp', 'expert')), may hold values from 0 to 255, all different within a row
- gating_shares: float32 [262144, 8], P(('dp', 'expert')), may hold values from 0.05 to 0.3
- seat_limits: int32 [64], replicated, may hold values from 4 to 8, as said below
- raising_factors: bfloat16 [64, 512, 1024], P('expert', 'dp'), may hold values from -0.25 to 0.25
- lowering_factors: bfloat16 [64, 512, 1024], P('expert', 'dp'), may hold values from -0.1875 to 0.1875
- result_cotangent: bfloat16 [262144, 512], P(('dp', 'expert')), may hold values from -6 to 6
Outputs:
- combined: bfloat16 [262144, 512], P(('dp', 'expert'))
- latent_grad: bfloat16 [262144, 512], P(('dp', 'expert'))
- prob_grad: float32 [262144, 8], P(('dp', 'expert'))
- up_weight_grad: float32 [64, 512, 1024], P('expert', 'dp')
- down_weight_grad: float32 [64, 512, 1024], P('expert', 'dp')
Inputs may be any that keep to these rules, and one draw needn't show every extreme that they name: `picked_specialists`: each row names 8 different experts; experts 64 and above are not in flight. `seat_limits`: at least one expert has capacity 8 and at least one has half of 8.
All inputs are finite; a program needn't handle non-finite values.
Results may differ from a plain program's by a relative error of at most 0.02.
Values may be sent and summed in bfloat16 or wider, within the bound.
A program may use at most 32 MiB of HBM per device.

v0:
```python
import jax
import jax.numpy as jnp
from jax import lax
from jax.sharding import PartitionSpec as P

CAP = 8


def assigned_seat(picked_specialists, seat_limits, specialist_seats):
    specialists_aloft = seat_limits.shape[0]
    flattened_ids = picked_specialists.reshape(-1)
    path_total = flattened_ids.shape[0]
    specialist_range = jnp.arange(specialists_aloft, dtype=jnp.int32)
    indicator_table = (flattened_ids[:, None] == specialist_range[None, :]).astype(jnp.int32)
    before = jnp.cumsum(indicator_table, axis=0, dtype=jnp.int32) - indicator_table
    ordinal_place = jnp.sum(before * indicator_table, axis=1, dtype=jnp.int32)
    seat_table = jnp.sum(indicator_table * seat_limits[None, :], axis=1, dtype=jnp.int32)
    admitted_flags = (flattened_ids < specialists_aloft) & (ordinal_place < seat_table)
    seat_number = jnp.where(
        admitted_flags,
        flattened_ids * specialist_seats + ordinal_place,
        specialists_aloft * specialist_seats,
    )
    seat_occupant = jnp.full((specialists_aloft * specialist_seats,), path_total, jnp.int32)
    seat_occupant = seat_occupant.at[seat_number].set(
        jnp.arange(path_total, dtype=jnp.int32), mode="drop"
    )
    return (
        admitted_flags,
        jnp.minimum(seat_number, specialists_aloft * specialist_seats - 1),
        seat_occupant,
    )


def pack_rows(values, row_index, filled):
    picked = values[jnp.minimum(row_index, values.shape[0] - 1)]
    return jnp.where(filled[:, None], picked, jnp.zeros_like(picked))


def shift_entries(entry_batch, specialists_aloft, specialist_seats):
    reformed_array = entry_batch.reshape(specialists_aloft, specialist_seats, entry_batch.shape[-1])
    landed_entries = lax.all_to_all(
        reformed_array, "expert", split_axis=0, concat_axis=0, tiled=True
    )
    return landed_entries.reshape(specialists_aloft * specialist_seats, entry_batch.shape[-1])


def body(
    compressed_tokens,
    picked_specialists,
    gating_shares,
    seat_limits,
    raising_factors,
    lowering_factors,
    result_cotangent,
):
    specialists_aloft = lax.axis_size("expert")
    specialist_seats = CAP
    tok_rows = picked_specialists.shape[0]
    top_count = picked_specialists.shape[1]
    path_total = tok_rows * top_count
    width = compressed_tokens.shape[1]
    admitted_flags, seat_number, seat_occupant = assigned_seat(
        picked_specialists, seat_limits, specialist_seats
    )
    filled = seat_occupant < path_total
    dispatch_entries = pack_rows(compressed_tokens, seat_occupant // top_count, filled)
    route_weight = jnp.where(admitted_flags, gating_shares.reshape(-1), 0.0)
    route_grad = (
        route_weight.reshape(tok_rows, top_count)[:, :, None]
        * result_cotangent.astype(jnp.float32)[:, None, :]
    )
    route_grad = route_grad.reshape(path_total, width).astype(jnp.bfloat16)
    cotangent_dispatch = pack_rows(route_grad, seat_occupant, filled)
    incoming_entries = shift_entries(dispatch_entries, specialists_aloft, specialist_seats)
    up_full, down_full = (
        lax.all_gather(raising_factors, "dp", axis=1, tiled=True),
        lax.all_gather(lowering_factors, "dp", axis=1, tiled=True),
    )
    up_matrix = up_full[0]
    down_matrix = down_full[0]
    preact = jnp.dot(incoming_entries, up_matrix, preferred_element_type=jnp.float32)
    active = jnp.maximum(preact, 0.0)
    hidden = (active * active).astype(jnp.bfloat16)
    specialist_result = lax.dot_general(
        hidden, down_matrix, (((1,), (1,)), ((), ())), preferred_element_type=jnp.float32
    ).astype(jnp.bfloat16)
    homeward_entries = shift_entries(specialist_result, specialists_aloft, specialist_seats)
    cotangent_entering = shift_entries(cotangent_dispatch, specialists_aloft, specialist_seats)
    hidden_grad = jnp.dot(cotangent_entering, down_matrix, preferred_element_type=jnp.float32)
    act_grad = (2.0 * active * hidden_grad).astype(jnp.bfloat16)
    entry_cotangent = lax.dot_general(
        act_grad, up_matrix, (((1,), (1,)), ((), ())), preferred_element_type=jnp.float32
    ).astype(jnp.bfloat16)
    cotangent_return = shift_entries(entry_cotangent, specialists_aloft, specialist_seats)
    route_out = homeward_entries[seat_number]
    combined = jnp.sum(
        (route_weight[:, None] * route_out.astype(jnp.float32)).reshape(tok_rows, top_count, width),
        axis=1,
    )
    combined = combined.astype(jnp.bfloat16)
    dots = jnp.einsum(
        "tl,tkl->tk",
        result_cotangent,
        route_out.reshape(tok_rows, top_count, width),
        preferred_element_type=jnp.float32,
    )
    prob_grad = jnp.where(admitted_flags.reshape(tok_rows, top_count), dots, 0.0)
    route_dx = cotangent_return[seat_number].astype(jnp.float32) * admitted_flags[:, None].astype(
        jnp.float32
    )
    latent_grad = jnp.sum(route_dx.reshape(tok_rows, top_count, width), axis=1).astype(jnp.bfloat16)
    up_term = lax.dot_general(
        incoming_entries, act_grad, (((0,), (0,)), ((), ())), preferred_element_type=jnp.float32
    )
    down_term = lax.dot_general(
        cotangent_entering, hidden, (((0,), (0,)), ((), ())), preferred_element_type=jnp.float32
    )
    up_grad, down_grad = (
        lax.psum_scatter(
            up_term.astype(jnp.bfloat16), "dp", scatter_dimension=0, tiled=True
        ).astype(jnp.float32),
        lax.psum_scatter(
            down_term.astype(jnp.bfloat16), "dp", scatter_dimension=0, tiled=True
        ).astype(jnp.float32),
    )
    return (combined, latent_grad, prob_grad, up_grad[None], down_grad[None])


def solution(mesh):
    in_specs = (
        P(("dp", "expert"), None),
        P(("dp", "expert"), None),
        P(("dp", "expert"), None),
        P(),
        P("expert", "dp", None),
        P("expert", "dp", None),
        P(("dp", "expert"), None),
    )
    out_specs = (
        P(("dp", "expert"), None),
        P(("dp", "expert"), None),
        P(("dp", "expert"), None),
        P("expert", "dp", None),
        P("expert", "dp", None),
    )
    return jax.shard_map(body, mesh=mesh, in_specs=in_specs, out_specs=out_specs, check_vma=False)
```

profile of v0, /device:TPU:48, one launch (start us, length us, event | category | flops | bytes accessed | tf_op | source)
XLA Modules:
  0.0 512.3 jit_solution(7907582892256326299)
XLA Ops:
  10.0 18.1 %reduce-window.6 = s32[64,16,128]{2,1,0:T(8,128)S(1)} reduce-window(s32[64,16,128]{2,1,0:T(8,128)S(1)} %fusion.19, s32[]{:T(128)} %constant.17.clone.1), window={size=1x1x128 pad=0_0x0_0x127_0}, to_apply=%region_0.0 | reduce-window | flops 16646144 | bytes 1048580 | tf_op jit(solution)/shard_map/reduce-window
  31.1 8.0 %scatter_custom_fusion = s32[512]{0:T(512)S(1)} fusion(s32[2048]{0:T(1024)S(1)} %bitcast.86, s32[2048]{0:T(1024)S(1)} %iota.11, s32[]{:T(128)} %constant.19.clone.1), kind=kCustom, calls=%fused_computation.64 | custom fusion | bytes 2052 | tf_op jit(solution)/shard_map/scatter | solution.py:25
  39.9 2.0 gather_fusion
  42.8 24.6 %all-to-all-start = ((bf16[64,8,512]{2,1,0:T(8,128)(2,1)}), bf16[64,8,512]{2,1,0:T(8,128)(2,1)S(1)}, u32[]{:S(2)}, u32[]{:S(2)}) async-start(bf16[64,8,512]{2,1,0:T(8,128)(2,1)} %bitcast_select_fusion.1), calls=%async_computation | async-start | bytes 1048576 | tf_op jit(solution)/shard_map/all_to_all | solution.py:42
  68.2 47.3 %all-gather.3.cloned.1.call-done = bf16[1,512,1024]{2,1,0:T(8,128)(2,1)} async-done(((bf16[1,32,1024]{2,1,0:T(8,128)(2,1)}), bf16[1,512,1024]{2,1,0:T(8,128)(2,1)}) %all-gather.3.cloned.1.call-update) | async-done | bytes 1048592 | tf_op jit(solution)/shard_map/all_gather | solution.py:77
  115.5 2.1 fusion.9
  117.6 87.6 %all-gather.5.cloned.1.call-done = bf16[1,512,1024]{2,1,0:T(8,128)(2,1)} async-done(((bf16[1,32,1024]{2,1,0:T(8,128)(2,1)}), bf16[1,512,1024]{2,1,0:T(8,128)(2,1)}) %all-gather.5.cloned.1.call-update) | async-done | bytes 1048592 | tf_op jit(solution)/shard_map/all_gather | solution.py:78
  205.2 2.8 fusion.4
  207.9 18.0 %all-to-all-start.1 = ((bf16[64,8,512]{2,1,0:T(8,128)(2,1)}), bf16[64,8,512]{2,1,0:T(8,128)(2,1)S(1)}, u32[]{:S(2)}, u32[]{:S(2)}) async-start(bf16[64,8,512]{2,1,0:T(8,128)(2,1)} %fusion.4), calls=%async_computation.1 | async-start | bytes 1048576 | tf_op jit(solution)/shard_map/all_to_all | solution.py:42
  228.5 23.5 %all-to-all-done.1 = bf16[64,8,512]{2,1,0:T(8,128)(2,1)S(1)} async-done(((bf16[64,8,512]{2,1,0:T(8,128)(2,1)}), bf16[64,8,512]{2,1,0:T(8,128)(2,1)S(1)}, u32[]{:S(2)}, u32[]{:S(2)}) %all-to-all-start.1) | async-done | bytes 524320 | tf_op jit(solution)/shard_map/all_to_all | solution.py:42
  252.0 9.2 %gather_fusion.1 = bf16[2048,512]{1,0:T(8,128)(2,1)} fusion(bf16[512,512]{1,0:T(8,128)(2,1)S(1)} %bitcast.77, s32[2048]{0:T(1024)S(1)} %broadcast_clamp_fusion), kind=kCustom, calls=%fused_computation.1 | custom fusion | bytes 4202496 | tf_op jit(solution)/shard_map/gather | solution.py:96
  261.2 2.6 fusion.2
  266.3 3.8 gather_fusion.2
  270.3 40.7 %all_to_all.20 = bf16[64,8,512]{2,1,0:T(8,128)(2,1)S(1)} all-to-all(bf16[64,8,512]{2,1,0:T(8,128)(2,1)S(1)} %bitcast_select_fusion), channel_id=1, replica_groups=mesh['dp'=16,'expert'=64] {'expert'}, dimensions={0} | all-to-all | bytes 1048576 | tf_op jit(solution)/shard_map/all_to_all | solution.py:42
  312.8 1.7 convolution_convert_fusion.1
  314.6 3.1 fusion.5
  317.7 11.0 %all-to-all-start.3 = ((bf16[64,8,512]{2,1,0:T(8,128)(2,1)}), bf16[64,8,512]{2,1,0:T(8,128)(2,1)S(1)}, u32[]{:S(2)}, u32[]{:S(2)}) async-start(bf16[64,8,512]{2,1,0:T(8,128)(2,1)} %fusion.5), calls=%async_computation.3 | async-start | bytes 1048576 | tf_op jit(solution)/shard_map/all_to_all | solution.py:42
  328.7 1.7 convolution_convert_fusion
  332.1 3.7 multiply_reduce_fusion
  335.7 24.1 %all-to-all-done.3 = bf16[64,8,512]{2,1,0:T(8,128)(2,1)S(1)} async-done(((bf16[64,8,512]{2,1,0:T(8,128)(2,1)}), bf16[64,8,512]{2,1,0:T(8,128)(2,1)S(1)}, u32[]{:S(2)}, u32[]{:S(2)}) %all-to-all-start.3) | async-done | bytes 524320 | tf_op jit(solution)/shard_map/all_to_all | solution.py:42
  359.8 7.5 %gather_fusion.3 = bf16[2048,512]{1,0:T(8,128)(2,1)S(1)} fusion(bf16[512,512]{1,0:T(8,128)(2,1)S(1)} %bitcast.76, s32[2048]{0:T(1024)S(1)} %broadcast_clamp_fusion), kind=kCustom, calls=%fused_computation.3 | custom fusion | bytes 4202496 | tf_op jit(solution)/shard_map/gather | solution.py:109
  367.3 2.0 fusion
  369.3 39.8 %reduce-scatter.3.cloned.1.call-done = bf16[32,1024]{1,0:T(8,128)(2,1)} async-done(((bf16[512,1024]{1,0:T(8,128)(2,1)}), bf16[32,1024]{1,0:T(8,128)(2,1)}) %reduce-scatter.3.cloned.1.call-update) | async-done | bytes 65552 | tf_op jit(solution)/shard_map/reduce_scatter | solution.py:120
  410.6 93.7 %reduce-scatter.5.cloned.1.call-done = bf16[32,1024]{1,0:T(8,128)(2,1)} async-done(((bf16[512,1024]{1,0:T(8,128)(2,1)}), bf16[32,1024]{1,0:T(8,128)(2,1)}) %reduce-scatter.5.cloned.1.call-update) | async-done | bytes 65552 | tf_op jit(solution)/shard_map/reduce_scatter | solution.py:123
  (72 shorter events, 19.6 us)
Async XLA Ops:
  7.2 32.7 %copy-start = (bf16[256,512]{1,0:T(8,128)(2,1)S(1)}, bf16[256,512]{1,0:T(8,128)(2,1)}, u32[]{:S(2)}) copy-start(bf16[256,512]{1,0:T(8,128)(2,1)} %param.7) | copy-start | bytes 786436
  7.2 108.3 %all-gather.3.cloned.1.call-start = ((), (), s32[]{:S(2)}) async-start(), calls=%async_computation.6 | async-start | bytes 1114112 | tf_op jit(solution)/shard_map/all_gather | solution.py:77
  9.9 19.2 %copy-start.13 = (s32[64]{0:T(128)S(1)}, s32[64]{0:T(128)}, u32[]{:S(2)}) copy-start(s32[64]{0:T(128)} %param.10) | copy-start | bytes 772
  29.6 10.3 %copy-start.9 = (pred[256,8]{1,0:T(8,128)(4,1)}, pred[256,8]{1,0:T(8,128)(4,1)S(1)}, u32[]{:S(2)}) copy-start(pred[256,8]{1,0:T(8,128)(4,1)S(1)} %lt.90) | copy-start | bytes 6148
  30.3 9.6 %copy-start.7 = (pred[256,8]{1,0:T(8,128)(4,1)}, pred[256,8]{1,0:T(8,128)(4,1)S(1)}, u32[]{:S(2)}) copy-start(pred[256,8]{1,0:T(8,128)(4,1)S(1)} %get-tuple-element.13) | copy-start | bytes 6148
  42.8 72.7 %all-to-all-start = ((bf16[64,8,512]{2,1,0:T(8,128)(2,1)}), bf16[64,8,512]{2,1,0:T(8,128)(2,1)S(1)}, u32[]{:S(2)}, u32[]{:S(2)}) async-start(bf16[64,8,512]{2,1,0:T(8,128)(2,1)} %bitcast_select_fusion.1), calls=%async_computation | async-start | bytes 1048576 | tf_op jit(solution)/shard_map/all_to_all | solution.py:42
  67.4 137.7 %all-gather.5.cloned.1.call-start = ((), (), s32[]{:S(2)}) async-start(), calls=%async_computation.7 | async-start | bytes 1114112 | tf_op jit(solution)/shard_map/all_gather | solution.py:78
  115.5 92.5 %copy-start.2 = (bf16[64,8,512]{2,1,0:T(8,128)(2,1)}, bf16[64,8,512]{2,1,0:T(8,128)(2,1)S(1)}, u32[]{:S(2)}) copy-start(bf16[64,8,512]{2,1,0:T(8,128)(2,1)S(1)} %all-to-all-done) | copy-start | bytes 1572868
  117.6 108.4 %copy-start.12 = (f32[256,8]{0,1:T(8,128)S(1)}, f32[256,8]{0,1:T(8,128)}, u32[]{:S(2)}) copy-start(f32[256,8]{0,1:T(8,128)} %param.9) | copy-start | bytes 24580
  207.9 44.1 %all-to-all-start.1 = ((bf16[64,8,512]{2,1,0:T(8,128)(2,1)}), bf16[64,8,512]{2,1,0:T(8,128)(2,1)S(1)}, u32[]{:S(2)}, u32[]{:S(2)}) async-start(bf16[64,8,512]{2,1,0:T(8,128)(2,1)} %fusion.4), calls=%async_computation.1 | async-start | bytes 1048576 | tf_op jit(solution)/shard_map/all_to_all | solution.py:42
  225.9 183.2 %reduce-scatter.3.cloned.1.call-start = ((), (), s32[]{:S(2)}) async-start(), calls=%async_computation.8 | async-start | bytes 1114112 | tf_op jit(solution)/shard_map/reduce_scatter | solution.py:120
  261.2 2.6 copy-start.6
  261.2 2.6 copy-start.8
  261.2 2.6 copy-start.10
  263.8 2.5 copy-start.11
  270.2 40.9 %copy-start.1 = (bf16[1,512,1024]{2,1,0:T(8,128)(2,1)S(1)}, bf16[1,512,1024]{2,1,0:T(8,128)(2,1)}, u32[]{:S(2)}) copy-start(bf16[1,512,1024]{2,1,0:T(8,128)(2,1)} %all-gather.5.cloned.1.call-done) | copy-start | bytes 3145732
  311.1 1.8 copy-start.3
  311.8 1.0 copy-start.4
  317.7 42.1 %all-to-all-start.3 = ((bf16[64,8,512]{2,1,0:T(8,128)(2,1)}), bf16[64,8,512]{2,1,0:T(8,128)(2,1)S(1)}, u32[]{:S(2)}, u32[]{:S(2)}) async-start(bf16[64,8,512]{2,1,0:T(8,128)(2,1)} %fusion.5), calls=%async_computation.3 | async-start | bytes 1048576 | tf_op jit(solution)/shard_map/all_to_all | solution.py:42
  328.7 175.6 %reduce-scatter.5.cloned.1.call-start = ((), (), s32[]{:S(2)}) async-start(), calls=%async_computation.9 | async-start | bytes 1114112 | tf_op jit(solution)/shard_map/reduce_scatter | solution.py:123
  359.8 7.5 %copy-start.5 = (f32[256,8]{1,0:T(8,128)S(1)}, f32[256,8]{1,0:T(8,128)}, u32[]{:S(2)}) copy-start(f32[256,8]{1,0:T(8,128)} %get-tuple-element.12) | copy-start | bytes 24580
Sparse Core Ops, SparseCore 0:
  10.7 104.7 all-gather.2
  118.1 87.0 all-gather.4
  314.7 94.4 reduce-scatter.2
  412.7 91.5 reduce-scatter.4
where the time goes:
time: 514 us; the launch traced here: 512 us
  waiting for transfers between devices  317 us (62%)
  starting transfers between devices  53.8 us (10%)
  blocking collectives  40.7 us (8%)
  local copies, waits for them, and re-layouts  36.3 us (7%)
  other arithmetic  35.3 us (7%)
  matrix products  14.8 us (3%)
  between operations  14 us (3%)
    reduce_scatter x1, waiting for transfers between devices, body(): lax.psum_scatter(down_term.astype(jnp.bfloat16), 'dp', scatter_dimension=...  93.7 us
    all_gather x1, waiting for transfers between devices, body(): lax.all_gather(lowering_factors, 'dp', axis=1, tiled=True)  87.6 us
    all_to_all x3, starting transfers between devices, shift_entries(): lax.all_to_all(reformed_array, 'expert', split_axis=0, concat_axis=0, til...  53.6 us
    all_to_all x3, waiting for transfers between devices, shift_entries(): lax.all_to_all(reformed_array, 'expert', split_axis=0, concat_axis=0, til...  47.6 us
    all_gather x1, waiting for transfers between devices, body(): lax.all_gather(raising_factors, 'dp', axis=1, tiled=True)  47.3 us
    all_to_all x1, blocking collectives, shift_entries(): lax.all_to_all(reformed_array, 'expert', split_axis=0, concat_axis=0, til...  40.7 us
    reduce_scatter x1, waiting for transfers between devices, body(): lax.psum_scatter(up_term.astype(jnp.bfloat16), 'dp', scatter_dimension=0,...  39.8 us
    another operation x3, other arithmetic  18.5 us
  transfers between devices with their start and end apart: 7, of which 6 were waited for; matrix products, arithmetic and copies ran while one was open for 12% of the time, Pallas kernels for 0%

commit v1 on v0

v1 whole, which is shorter than its diff:
```python
import functools

import jax
import jax.numpy as jnp
from jax import lax
from jax.experimental import pallas as pl
from jax.experimental.pallas import tpu as pltpu
from jax.sharding import PartitionSpec as P

DP_GRID = (4, 4)
EXPERT_GRID = (8, 4, 2)
SEATS = 8
PAIR = 2 * SEATS
COLUMNS = 256
MESH = pl.DeviceIdType.MESH
BF16 = jnp.bfloat16
F32 = jnp.float32


def dot(a, b):
    return jnp.dot(a, b, preferred_element_type=F32)


def dot_nt(a, b):
    return lax.dot_general(a, b, (((1,), (1,)), ((), ())), preferred_element_type=F32)


def dot_tn(a, b):
    return lax.dot_general(a, b, (((0,), (0,)), ((), ())), preferred_element_type=F32)


def parts_of(values):
    first = values.astype(BF16)
    rest = values - first.astype(F32)
    second = rest.astype(BF16)
    third = (rest - second.astype(F32)).astype(BF16)
    return first, second, third


def paired(upper, lower, blocks):
    width = upper.shape[-1]
    return jnp.concatenate(
        [upper.reshape(blocks, SEATS, width), lower.reshape(blocks, SEATS, width)], axis=1
    ).astype(BF16)


def unpaired(blocks):
    count, _, width = blocks.shape
    wide = blocks.astype(F32)
    return (
        wide[:, :SEATS].reshape(count * SEATS, width),
        wide[:, SEATS:].reshape(count * SEATS, width),
    )


def kernel(
    tok_ref, pick_ref, share_ref, limit_ref, up_ref, down_ref, cot_ref,
    comb_ref, lat_ref, prob_ref, up_grad_ref, down_grad_ref,
    weights, outbox, inbox, reply, home, place, cot_rows, row_share,
    xs, gs, hs, acts, partial, x_in, z_out, z_in,
    ag_z_send, ag_z_recv, ag_x_send, ag_x_recv,
    row_send, row_recv, back_send, back_recv, self_sem,
    rs_x_send, rs_x_recv, rs_z_send, rs_z_recv,
):
    runs, wide = DP_GRID
    ys, stretches, cores = EXPERT_GRID
    experts = ys * stretches * cores
    members = ys * cores
    tokens, lat = tok_ref.shape
    top = pick_ref.shape[1]
    hid = weights.shape[-1]
    slots = experts * SEATS
    group_rows = members * SEATS

    dp = lax.axis_index("dp")
    me = lax.axis_index("expert")
    run, across = dp // wide, dp % wide
    my_y = me // (stretches * cores)
    my_stretch = (me // cores) % stretches
    my_core = me % cores
    my_member = my_y * cores + my_core

    def run_peer(j):
        return {"dp": lax.rem(run + j, runs) * wide + across}

    def wide_peer(j):
        return {"dp": run * wide + lax.rem(across + j, wide)}

    def expert_at(stretch_step, member_step):
        stretch = lax.rem(my_stretch + stretch_step, stretches)
        member = lax.rem(my_member + member_step, members)
        return ((member // cores) * stretches + stretch) * cores + lax.rem(member, cores), member

    barrier = pltpu.get_barrier_semaphore()

    def greet(i, carry):
        pl.semaphore_signal(
            barrier, inc=1, device_id={"expert": lax.rem(me + i, experts)}, device_id_type=MESH
        )
        return carry

    for j in range(1, runs):
        pl.semaphore_signal(barrier, inc=1, device_id=run_peer(j), device_id_type=MESH)
    for j in range(1, wide):
        pl.semaphore_signal(barrier, inc=1, device_id=wide_peer(j), device_id_type=MESH)
    lax.fori_loop(1, experts, greet, 0)

    weights[0, run, across] = up_ref[0]
    weights[1, run, across] = down_ref[0]

    picks = pick_ref[...]
    shares = share_ref[...]
    expert_lane = lax.broadcasted_iota(jnp.int32, (tokens, experts), 1)
    named = jnp.zeros((tokens, experts), F32)
    weight = jnp.zeros((tokens, experts), F32)
    for k in range(top):
        hit = picks[:, k : k + 1] == expert_lane
        named = jnp.where(hit, 1.0, named)
        weight = jnp.where(hit, shares[:, k : k + 1], weight)
    earlier = (
        lax.broadcasted_iota(jnp.int32, (tokens, tokens), 1)
        < lax.broadcasted_iota(jnp.int32, (tokens, tokens), 0)
    ).astype(BF16)
    position = dot(earlier, named.astype(BF16))
    seated = (named > 0.0) & (position < limit_ref[...].astype(F32))
    seat = jnp.where(seated, position, -1.0).astype(BF16)
    spread = (
        lax.broadcasted_iota(jnp.int32, (experts, slots), 1) // SEATS
        == lax.broadcasted_iota(jnp.int32, (experts, slots), 0)
    ).astype(BF16)
    slot_seat = (lax.broadcasted_iota(jnp.int32, (tokens, slots), 1) % SEATS).astype(F32)
    place[...] = (dot(seat, spread) == slot_seat).astype(BF16)
    slot_expert = (
        lax.broadcasted_iota(jnp.int32, (slots, experts), 0) // SEATS
        == lax.broadcasted_iota(jnp.int32, (slots, experts), 1)
    )

    pl.semaphore_wait(barrier, experts - 1 + runs - 1 + wide - 1)

    z_copies = []
    for j in range(1, runs):
        copy = pltpu.make_async_remote_copy(
            src_ref=weights.at[:, run, across],
            dst_ref=weights.at[:, run, across],
            send_sem=ag_z_send.at[j],
            recv_sem=ag_z_recv.at[j],
            device_id=run_peer(j),
            device_id_type=MESH,
        )
        copy.start()
        z_copies.append(copy)

    def fan_out(block):
        for j in range(1, wide):
            pltpu.make_async_remote_copy(
                src_ref=weights.at[:, block, across],
                dst_ref=weights.at[:, block, across],
                send_sem=ag_x_send,
                recv_sem=ag_x_recv,
                device_id=wide_peer(j),
                device_id_type=MESH,
            ).start()

    fan_out(run)

    x_rows = dot_tn(place[...], tok_ref[...])
    c_rows = dot_tn(place[...], cot_ref[...])
    cot_rows[...] = c_rows.astype(BF16)
    per_expert = sum(dot_tn(place[...], part) for part in parts_of(weight))
    slot_share = jnp.sum(jnp.where(slot_expert, per_expert, 0.0), axis=1, keepdims=True)
    row_share[...] = slot_share
    outbox[...] = paired(x_rows, slot_share * c_rows, experts)

    own_rows = pltpu.make_async_copy(outbox.at[me], inbox.at[0, my_member], self_sem.at[0])
    own_rows.start()

    def send_rows(step, first):
        def send(i, carry):
            peer, _ = expert_at(step, i)
            pltpu.make_async_remote_copy(
                src_ref=outbox.at[peer],
                dst_ref=inbox.at[(stretches - step) % stretches, my_member],
                send_sem=row_send,
                recv_sem=row_recv.at[(stretches - step) % stretches],
                device_id={"expert": peer},
                device_id_type=MESH,
            ).start()
            return carry

        lax.fori_loop(first, members, send, 0)

    far_first = sorted(range(1, stretches), key=lambda s: -min(s, stretches - s))
    for step in far_first:
        send_rows(step, 0)
    send_rows(0, 1)

    for j in range(1, runs):
        z_copies[j - 1].wait_recv()
        fan_out(lax.rem(run + runs - j, runs))
    blocks_in = weights.at[:, :, pl.ds(0, wide - 1)]
    pltpu.make_async_copy(blocks_in, blocks_in, ag_x_recv).wait()

    def wait_bytes(ref, sem):
        pltpu.make_async_copy(ref, ref, sem).wait()

    own_back = None
    for step in [0] + far_first[::-1]:
        if step == 0:
            own_rows.wait()
            wait_bytes(inbox.at[0, pl.ds(0, members - 1)], row_recv.at[0])
        else:
            wait_bytes(inbox.at[step], row_recv.at[step])
        rows = pl.ds(step * group_rows, group_rows)
        x_f32, g_f32 = unpaired(inbox[step])
        x = x_f32.astype(BF16)
        g = g_f32.astype(BF16)
        xs[rows] = x
        gs[rows] = g
        for column in range(0, hid, COLUMNS):
            columns = pl.ds(column, COLUMNS)
            active = jnp.maximum(dot(x, weights[0, :, :, :, columns].reshape(lat, COLUMNS)), 0.0)
            hidden_grad = dot(g, weights[1, :, :, :, columns].reshape(lat, COLUMNS))
            hs[rows, columns] = (active * active).astype(BF16)
            acts[rows, columns] = (2.0 * active * hidden_grad).astype(BF16)
        out = dot_nt(hs[rows], weights[1].reshape(lat, hid))
        row_grad = dot_nt(acts[rows], weights[0].reshape(lat, hid))
        reply[step] = paired(out, row_grad, members)

        if step == 0:
            own_back = pltpu.make_async_copy(
                reply.at[0, my_member], home.at[me], self_sem.at[1]
            )
            own_back.start()

        def send_back(i, carry, step=step):
            peer, member = expert_at(step, i)
            pltpu.make_async_remote_copy(
                src_ref=reply.at[step, member],
                dst_ref=home.at[me],
                send_sem=back_send,
                recv_sem=back_recv,
                device_id={"expert": peer},
                device_id_type=MESH,
            ).start()
            return carry

        lax.fori_loop(1 if step == 0 else 0, members, send_back, 0)

    for w, (left, right) in enumerate(((xs, acts), (gs, hs))):
        for column in range(0, hid, COLUMNS):
            columns = pl.ds(column, COLUMNS)
            term = dot_tn(left[...], right[:, columns])
            partial[w, :, :, :, columns] = term.reshape(runs, wide, -1, COLUMNS).astype(BF16)
        for j in range(1, wide):
            there = lax.rem(across + j, wide)
            pltpu.make_async_remote_copy(
                src_ref=partial.at[w, :, there],
                dst_ref=x_in.at[w, j - 1],
                send_sem=rs_x_send.at[w],
                recv_sem=rs_x_recv.at[w],
                device_id=wide_peer(j),
                device_id_type=MESH,
            ).start()
    for w in range(2):
        wait_bytes(x_in.at[w], rs_x_recv.at[w])
        total = partial[w, :, across].astype(F32)
        for j in range(wide - 1):
            total += x_in[w, j].astype(F32)
        z_out[w] = total.astype(BF16)
        for j in range(1, runs):
            pltpu.make_async_remote_copy(
                src_ref=z_out.at[w, lax.rem(run + j, runs)],
                dst_ref=z_in.at[w, j - 1],
                send_sem=rs_z_send.at[w],
                recv_sem=rs_z_recv.at[w],
                device_id=run_peer(j),
                device_id_type=MESH,
            ).start()
    for w, grad_ref in enumerate((up_grad_ref, down_grad_ref)):
        wait_bytes(z_in.at[w], rs_z_recv.at[w])
        total = z_out[w, run].astype(F32)
        for j in range(runs - 1):
            total += z_in[w, j].astype(F32)
        grad_ref[0] = total

    own_back.wait()
    wait_bytes(home.at[pl.ds(0, experts - 1)], back_recv)
    out, row_grad = unpaired(home[...])
    share = row_share[...]
    lat_ref[...] = dot(place[...], row_grad.astype(BF16)).astype(BF16)
    first, second, _ = parts_of(share * out)
    comb_ref[...] = (dot(place[...], first) + dot(place[...], second)).astype(BF16)
    row_prob = jnp.sum(cot_rows[...].astype(F32) * out, axis=1, keepdims=True)
    by_expert = sum(
        dot(place[...], part) for part in parts_of(jnp.where(slot_expert, row_prob, 0.0))
    )
    rank_lane = lax.broadcasted_iota(jnp.int32, (tokens, top), 1)
    prob = jnp.zeros((tokens, top), F32)
    for k in range(top):
        hit = picks[:, k : k + 1] == expert_lane
        value = jnp.sum(jnp.where(hit, by_expert, 0.0), axis=1, keepdims=True)
        prob = jnp.where(rank_lane == k, value, prob)
    prob_ref[...] = prob

    for copy in z_copies:
        copy.wait_send()
    wait_bytes(blocks_in, ag_x_send)
    wait_bytes(outbox.at[pl.ds(0, experts - 1)], row_send)
    wait_bytes(home.at[pl.ds(0, experts - 1)], back_send)
    for w in range(2):
        wait_bytes(x_in.at[w], rs_x_send.at[w])
        wait_bytes(z_in.at[w], rs_z_send.at[w])


def body(
    compressed_tokens,
    picked_specialists,
    gating_shares,
    seat_limits,
    raising_factors,
    lowering_factors,
    result_cotangent,
):
    runs, wide = DP_GRID
    ys, stretches, cores = EXPERT_GRID
    experts = ys * stretches * cores
    members = ys * cores
    tokens, lat = compressed_tokens.shape
    top = picked_specialists.shape[1]
    _, depth, hid = raising_factors.shape
    slots = experts * SEATS
    vmem = pl.BlockSpec(memory_space=pltpu.VMEM)
    dma = pltpu.SemaphoreType.DMA
    return pl.pallas_call(
        kernel,
        out_shape=(
            jax.ShapeDtypeStruct((tokens, lat), BF16),
            jax.ShapeDtypeStruct((tokens, lat), BF16),
            jax.ShapeDtypeStruct((tokens, top), F32),
            jax.ShapeDtypeStruct((1, depth, hid), F32),
            jax.ShapeDtypeStruct((1, depth, hid), F32),
        ),
        in_specs=[vmem] * 7,
        out_specs=[vmem] * 5,
        scratch_shapes=[
            pltpu.VMEM((2, runs, wide, depth, hid), BF16),
            pltpu.VMEM((experts, PAIR, lat), BF16),
            pltpu.VMEM((stretches, members, PAIR, lat), BF16),
            pltpu.VMEM((stretches, members, PAIR, lat), BF16),
            pltpu.VMEM((experts, PAIR, lat), BF16),
            pltpu.VMEM((tokens, slots), BF16),
            pltpu.VMEM((slots, lat), BF16),
            pltpu.VMEM((slots, 1), F32),
            pltpu.VMEM((slots, lat), BF16),
            pltpu.VMEM((slots, lat), BF16),
            pltpu.VMEM((slots, hid), BF16),
            pltpu.VMEM((slots, hid), BF16),
            pltpu.VMEM((2, runs, wide, depth, hid), BF16),
            pltpu.VMEM((2, wide - 1, runs, depth, hid), BF16),
            pltpu.VMEM((2, runs, depth, hid), BF16),
            pltpu.VMEM((2, runs - 1, depth, hid), BF16),
            dma((runs,)),
            dma((runs,)),
            dma,
            dma,
            dma,
            dma((stretches,)),
            dma,
            dma,
            dma((2,)),
            dma((2,)),
            dma((2,)),
            dma((2,)),
            dma((2,)),
        ],
        compiler_params=pltpu.CompilerParams(
            collective_id=0, has_side_effects=True, vmem_limit_bytes=48 * 1024 * 1024
        ),
        name="moe_layer",
    )(
        compressed_tokens,
        picked_specialists,
        gating_shares,
        seat_limits.reshape(1, -1),
        raising_factors,
        lowering_factors,
        result_cotangent,
    )


def solution(mesh):
    in_specs = (
        P(("dp", "expert"), None),
        P(("dp", "expert"), None),
        P(("dp", "expert"), None),
        P(),
        P("expert", "dp", None),
        P("expert", "dp", None),
        P(("dp", "expert"), None),
    )
    out_specs = (
        P(("dp", "expert"), None),
        P(("dp", "expert"), None),
        P(("dp", "expert"), None),
        P("expert", "dp", None),
        P("expert", "dp", None),
    )
    return jax.shard_map(body, mesh=mesh, in_specs=in_specs, out_specs=out_specs, check_vma=False)
```

time: 514 us -> 156 us (0.30)
  the two profiles are of different devices: /device:TPU:48 before, /device:TPU:1 now
where the time goes in v1:
time: 156 us; the launch traced here: 155 us
  Pallas kernels  146 us (94%)
  local copies, waits for them, and re-layouts  7.7 us (5%)
    pallas_call x1, Pallas kernels, body(): pl.pallas_call(kernel, out_shape=(jax.ShapeDtypeStruct((tokens, lat), BF1...  146 us
    unnamed x16, local copies, waits for them, and re-layouts  7.03 us

profile of v1, /device:TPU:1, one launch (start us, length us, event | category | flops | bytes accessed | tf_op | source)
XLA Modules:
  0.0 154.6 jit_solution(16716787844670521566)
XLA Ops:
  0.6 0.0 copy-start
  0.6 0.9 copy.12.pick_ref
  1.5 0.0 copy-start.4
  1.5 0.8 copy.13.share_ref
  2.4 0.0 copy-done
  2.4 0.0 copy-done.4
  2.4 0.0 copy-start.1
  2.4 0.9 copy-done.1
  3.3 0.0 copy-start.2
  3.3 0.8 copy-done.2
  4.2 0.0 copy-start.3
  4.2 0.8 copy-done.3
  5.0 146.2 %moe_layer.1 = (bf16[256,512]{1,0:T(8,128)(2,1)S(1)}, bf16[256,512]{1,0:T(8,128)(2,1)S(1)}, f32[256,8]{1,0:T(8,128)S(1)}, f32[1,32,1024]{2,1,0:T(8,128)S(1)}, f32[1,32,1024]{2,1,0:T(8,128)S(1)}) custom-call(bf16[256,512]{1,0:T(8,128)(2,1)S(1)} %copy-done, s32[256,8]{1,0:T(8,128)S(1)} %copy.12.pick_ref, f32[256,8]{1,0:T(8,128)S(1)} %copy.13.share_ref, ...), custom_call_target="tpu_custom_call" | custom-call | tf_op jit(solution)/shard_map/moe_layer/pallas_call | solution.py:334
  151.3 0.7 copy.14
  151.9 0.7 copy.19
  152.6 0.7 copy.20
  153.3 0.7 copy.21
  154.0 0.7 copy.22
Async XLA Ops:
  0.6 1.7 %copy-start = (bf16[256,512]{1,0:T(8,128)(2,1)S(1)}, bf16[256,512]{1,0:T(8,128)(2,1)}, u32[]{:S(2)}) copy-start(bf16[256,512]{1,0:T(8,128)(2,1)} %tok_ref.1) | copy-start | bytes 786436
  1.5 0.9 copy-start.4
  2.4 1.0 copy-start.1
  3.3 0.8 copy-start.2
  4.2 0.8 copy-start.3

commit v2 on v1

v2 whole, which is shorter than its diff:
```python
import functools

import jax
import jax.numpy as jnp
from jax import lax
from jax.experimental import pallas as pl
from jax.experimental.pallas import tpu as pltpu
from jax.sharding import PartitionSpec as P

DP_GRID = (4, 4)
EXPERT_GRID = (8, 4, 2)
SEATS = 8
ROOMS = (104, 112, 128)
PAIR = 2 * SEATS
COLUMNS = 256
CHUNKS = 2
MESH = pl.DeviceIdType.MESH
BF16 = jnp.bfloat16
F32 = jnp.float32


def dot(a, b):
    return jnp.dot(a, b, preferred_element_type=F32)


def dot_nt(a, b):
    return lax.dot_general(a, b, (((1,), (1,)), ((), ())), preferred_element_type=F32)


def dot_tn(a, b):
    return lax.dot_general(a, b, (((0,), (0,)), ((), ())), preferred_element_type=F32)


def parts_of(values):
    first = values.astype(BF16)
    rest = values - first.astype(F32)
    second = rest.astype(BF16)
    third = (rest - second.astype(F32)).astype(BF16)
    return first, second, third


def paired(upper, lower, blocks):
    width = upper.shape[-1]
    return jnp.concatenate(
        [upper.reshape(blocks, SEATS, width), lower.reshape(blocks, SEATS, width)], axis=1
    ).astype(BF16)


def unpaired(blocks):
    count, _, width = blocks.shape
    wide = blocks.astype(F32)
    return (
        wide[:, :SEATS].reshape(count * SEATS, width),
        wide[:, SEATS:].reshape(count * SEATS, width),
    )


def kernel(
    room,
    tok_hbm, cot_hbm, up_hbm, down_hbm, pick_hbm, share_hbm, limit_hbm,
    comb_ref, lat_ref, prob_ref, up_grad_ref, down_grad_ref,
    weights, tok, cot, pick_ref, share_ref, limit_ref, own_out, outbox, middle, inbox, reply, gather, packed, own_home, home,
    place, place_t, unfold, unfolded, cot_rows, row_share, xs, gs, hs, acts, partial, x_in, z_out, z_in,
    load_sem, ag_z_send, ag_z_recv, ag_x_send, ag_x_recv,
    out_z_send, out_z_recv, out_y_send, out_y_recv, out_self,
    back_y_send, back_y_recv, back_z_send, back_z_recv, back_self,
    rs_x_send, rs_x_recv, rs_z_send, rs_z_recv, turn_sem,
):
    runs, wide = DP_GRID
    ys, stretches, cores = EXPERT_GRID
    experts = ys * stretches * cores
    members = ys * cores
    tokens, lat = tok.shape
    top = pick_ref.shape[0]
    hid = weights.shape[-1]
    group_rows = members * SEATS
    near_slots = members * SEATS
    slots = place.shape[0]

    dp = lax.axis_index("dp")
    me = lax.axis_index("expert")
    run, across = dp // wide, dp % wide
    my_stretch = (me // cores) % stretches
    my_member = (me // (stretches * cores)) * cores + me % cores

    def run_peer(j):
        return {"dp": lax.rem(run + j, runs) * wide + across}

    def wide_peer(j):
        return {"dp": run * wide + lax.rem(across + j, wide)}

    def expert_of(stretch, member):
        return ((member // cores) * stretches + stretch) * cores + member % cores

    def member_peer(i):
        return {"expert": expert_of(my_stretch, lax.rem(my_member + i, members))}

    def stretch_peer(j):
        return {"expert": expert_of(lax.rem(my_stretch + j, stretches), my_member)}

    def steps_to(expert):
        member = expert // (stretches * cores) * cores + expert % cores
        return (
            (expert // cores + stretches - my_stretch) % stretches,
            (member + members - my_member) % members,
        )

    def remote(src, dst, send_sem, recv_sem, peer):
        return pltpu.make_async_remote_copy(
            src_ref=src, dst_ref=dst, send_sem=send_sem, recv_sem=recv_sem,
            device_id=peer, device_id_type=MESH,
        )

    def wait_bytes(ref, sem):
        pltpu.make_async_copy(ref, ref, sem).wait()

    loads = [
        pltpu.make_async_copy(src, dst, load_sem.at[i])
        for i, (src, dst) in enumerate(
            (
                (up_hbm.at[0], weights.at[0, run, across]),
                (down_hbm.at[0], weights.at[1, run, across]),
                (pick_hbm, pick_ref),
                (share_hbm, share_ref),
                (limit_hbm, limit_ref),
                (tok_hbm, tok),
                (cot_hbm, cot),
            )
        )
    ]
    for load in loads:
        load.start()

    barrier = pltpu.get_barrier_semaphore()
    peers = [run_peer(j) for j in range(1, runs)] + [wide_peer(j) for j in range(1, wide)]
    peers += [stretch_peer(j) for j in range(1, stretches)]
    for peer in peers:
        pl.semaphore_signal(barrier, inc=1, device_id=peer, device_id_type=MESH)

    def greet(i, carry):
        pl.semaphore_signal(barrier, inc=1, device_id=member_peer(i), device_id_type=MESH)
        return carry

    lax.fori_loop(1, members, greet, 0)

    for load in loads[2:5]:
        load.wait()

    picks = pick_ref[...]
    shares = share_ref[...]
    expert_row = lax.broadcasted_iota(jnp.int32, (experts, tokens), 0)
    named = jnp.zeros((experts, tokens), F32)
    weight = jnp.zeros((experts, tokens), F32)
    for k in range(top):
        hit = picks[k : k + 1] == expert_row
        named = jnp.where(hit, 1.0, named)
        weight = jnp.where(hit, shares[k : k + 1], weight)
    earlier = (
        lax.broadcasted_iota(jnp.int32, (tokens, tokens), 0)
        < lax.broadcasted_iota(jnp.int32, (tokens, tokens), 1)
    ).astype(BF16)
    position = dot(named.astype(BF16), earlier)
    square = lax.broadcasted_iota(jnp.int32, (experts, experts), 0) == lax.broadcasted_iota(
        jnp.int32, (experts, experts), 1
    )
    limit_row = limit_ref[...].astype(F32)
    limit = jnp.sum(jnp.where(square, limit_row, 0.0), axis=1, keepdims=True)
    seat = jnp.where((named > 0.0) & (position < limit), position, -1.0).astype(BF16)
    across_stretch, along_members = steps_to(lax.broadcasted_iota(jnp.int32, (1, experts), 1))
    down_stretch, down_members = steps_to(lax.broadcasted_iota(jnp.int32, (experts, 1), 0))
    ahead = (down_stretch == across_stretch) & (down_members < along_members)
    offset = jnp.sum(jnp.where(ahead, limit, 0.0), axis=0, keepdims=True)
    first_slot = jnp.where(
        across_stretch == 0,
        (along_members * SEATS).astype(F32),
        (near_slots + (across_stretch - 1) * room).astype(F32) + offset,
    )
    slot = lax.broadcasted_iota(jnp.int32, (slots, experts), 0).astype(F32)
    slot_expert = (slot >= first_slot) & (slot < first_slot + limit_row)
    taken = jnp.sum(jnp.where(slot_expert, 1.0, 0.0), axis=1, keepdims=True)
    slot_seat = jnp.sum(jnp.where(slot_expert, slot - first_slot, 0.0), axis=1, keepdims=True)
    slot_seat = jnp.where(taken > 0.0, slot_seat, -2.0)
    place[...] = (dot(slot_expert.astype(BF16), seat) == slot_seat).astype(BF16)
    row = lax.broadcasted_iota(jnp.int32, (members * PAIR, experts), 0)
    row_expert = (across_stretch == 0) & (along_members == row // PAIR)
    row_first = jnp.sum(jnp.where(row_expert, offset, 0.0), axis=1, keepdims=True)
    row_limit = jnp.sum(jnp.where(row_expert, limit_row, 0.0), axis=1, keepdims=True)
    row = lax.broadcasted_iota(jnp.int32, (members * PAIR, 1), 0)
    row_seat = (row % SEATS).astype(F32)
    row_source = jnp.where(
        row_seat < row_limit,
        ((row % PAIR) // SEATS * room).astype(F32) + row_first + row_seat,
        -1.0,
    )
    packed_row = lax.broadcasted_iota(jnp.int32, (members * PAIR, 2 * room), 1).astype(F32)
    unfold[...] = (packed_row == row_source).astype(BF16)

    loads[0].wait()
    loads[1].wait()
    pl.semaphore_wait(barrier, len(peers) + members - 1)

    z_copies = []
    own = weights.at[:, run, across]
    for j in range(1, runs):
        copy = remote(own, own, ag_z_send.at[j], ag_z_recv.at[j], run_peer(j))
        copy.start()
        z_copies.append(copy)

    def fan_out(block):
        for j in range(1, wide):
            part = weights.at[:, block, across]
            remote(part, part, ag_x_send, ag_x_recv, wide_peer(j)).start()

    fan_out(run)

    loads[5].wait()
    loads[6].wait()
    x_rows = dot(place[...], tok[...])
    c_rows = dot(place[...], cot[...])
    cot_rows[...] = c_rows.astype(BF16)
    per_expert = sum(dot_nt(place[...], part) for part in parts_of(weight))
    slot_share = jnp.sum(jnp.where(slot_expert, per_expert, 0.0), axis=1, keepdims=True)
    row_share[...] = slot_share
    g_rows = slot_share * c_rows
    own_out[...] = paired(x_rows[:near_slots], g_rows[:near_slots], members)
    for j in range(1, stretches):
        first = near_slots + (j - 1) * room
        outbox[j - 1] = jnp.concatenate(
            [x_rows[first : first + room], g_rows[first : first + room]], axis=0
        ).astype(BF16)

    def spread(source, there):
        pltpu.make_async_copy(source.at[0], inbox.at[there, 0], out_self.at[there]).start()

        def send(i, carry):
            remote(
                source.at[i], inbox.at[there, members - i],
                out_y_send, out_y_recv.at[there], member_peer(i),
            ).start()
            return carry

        lax.fori_loop(1, members, send, 0)

    spread(own_out, 0)

    for j in range(1, runs):
        z_copies[j - 1].wait_recv()
        fan_out(lax.rem(run + runs - j, runs))

    order = sorted(range(1, stretches), key=lambda j: min(j, stretches - j))
    near, far = order[:-1], order[-1]

    def set_out(j):
        remote(
            outbox.at[j - 1], middle.at[j - 1], out_z_send, out_z_recv.at[j], stretch_peer(j)
        ).start()

    def tell_run(turn):
        for j in range(1, runs):
            pl.semaphore_signal(
                turn_sem.at[turn], inc=1, device_id=run_peer(j), device_id_type=MESH
            )

    def wait_run(turn):
        pl.semaphore_wait(turn_sem.at[turn], runs - 1)

    tell_run(0)
    wait_run(0)
    for j in near:
        set_out(j)

    def arrive(j):
        wait_bytes(middle.at[j - 1], out_z_recv.at[j])

    def forward(j):
        blocks = dot(unfold[...], middle[j - 1]).astype(BF16)
        unfolded[j - 1] = blocks.reshape(unfolded.shape[1:])
        spread(unfolded.at[j - 1], (stretches - j) % stretches)

    def expert_step(there):
        pltpu.make_async_copy(inbox.at[there, 0], inbox.at[there, 0], out_self.at[there]).wait()
        wait_bytes(inbox.at[there, pl.ds(1, members - 1)], out_y_recv.at[there])
        rows = pl.ds(there * group_rows, group_rows)
        x_f32, g_f32 = unpaired(inbox[there])
        x = x_f32.astype(BF16)
        g = g_f32.astype(BF16)
        xs[rows] = x
        gs[rows] = g
        for column in range(0, hid, COLUMNS):
            columns = pl.ds(column, COLUMNS)
            active = jnp.maximum(dot(x, weights[0, :, :, :, columns].reshape(lat, COLUMNS)), 0.0)
            hidden_grad = dot(g, weights[1, :, :, :, columns].reshape(lat, COLUMNS))
            hs[rows, columns] = (active * active).astype(BF16)
            acts[rows, columns] = (2.0 * active * hidden_grad).astype(BF16)
        out = dot_nt(hs[rows], weights[1].reshape(lat, hid))
        row_grad = dot_nt(acts[rows], weights[0].reshape(lat, hid))
        reply[there] = paired(out, row_grad, members)
        target = own_home if there == 0 else gather.at[there - 1]
        pltpu.make_async_copy(reply.at[there, 0], target.at[0], back_self.at[there]).start()

        def send(i, carry):
            remote(
                reply.at[there, i], target.at[members - i],
                back_y_send, back_y_recv.at[there], member_peer(i),
            ).start()
            return carry

        lax.fori_loop(1, members, send, 0)

    def gathered(there):
        target = own_home if there == 0 else gather.at[there - 1]
        pltpu.make_async_copy(target.at[0], target.at[0], back_self.at[there]).wait()
        wait_bytes(target.at[pl.ds(1, members - 1)], back_y_recv.at[there])

    def go_home(there):
        gathered(there)
        rows = gather[there - 1].reshape(members * PAIR, lat)
        packed[there - 1] = dot_tn(unfold[...], rows).astype(BF16)
        j = stretches - there
        remote(
            packed.at[there - 1], home.at[j - 1],
            back_z_send, back_z_recv.at[j], stretch_peer(there),
        ).start()

    for j in near:
        arrive(j)
    tell_run(1)
    for j in near:
        forward(j)
    wait_run(1)
    set_out(far)
    place_t[...] = place[...].T
    blocks_in = weights.at[:, :, pl.ds(0, wide - 1)]
    wait_bytes(blocks_in, ag_x_recv)
    expert_step(0)
    for j in near:
        expert_step(stretches - j)
    arrive(far)
    forward(far)
    for j in near:
        go_home(stretches - j)
    expert_step(stretches - far)

    chunk_columns = hid // CHUNKS
    chunks = [
        (grad_ref, left, right, half * chunk_columns)
        for grad_ref, left, right in ((up_grad_ref, xs, acts), (down_grad_ref, gs, hs))
        for half in range(CHUNKS)
    ]
    for q, (_, left, right, start) in enumerate(chunks):
        for column in range(0, chunk_columns, COLUMNS):
            term = dot_tn(left[...], right[:, pl.ds(start + column, COLUMNS)])
            term = term.reshape(runs, wide, -1, COLUMNS).astype(BF16)
            partial[q, :, :, :, pl.ds(column, COLUMNS)] = term
        for j in range(1, wide):
            there = lax.rem(across + j, wide)
            remote(
                partial.at[q, :, there], x_in.at[q, j - 1],
                rs_x_send.at[q], rs_x_recv.at[q], wide_peer(j),
            ).start()
    for q in range(len(chunks)):
        wait_bytes(x_in.at[q], rs_x_recv.at[q])
        total = partial[q, :, across].astype(F32)
        for j in range(wide - 1):
            total += x_in[q, j].astype(F32)
        z_out[q] = total.astype(BF16)
        for j in range(1, runs):
            remote(
                z_out.at[q, lax.rem(run + j, runs)], z_in.at[q, j - 1],
                rs_z_send.at[q], rs_z_recv.at[q], run_peer(j),
            ).start()
        if q == 0:
            go_home(stretches - far)
    for q, (grad_ref, _, _, start) in enumerate(chunks):
        wait_bytes(z_in.at[q], rs_z_recv.at[q])
        total = z_out[q, run].astype(F32)
        for j in range(runs - 1):
            total += z_in[q, j].astype(F32)
        grad_ref[0, :, pl.ds(start, chunk_columns)] = total

    gathered(0)
    for j in range(1, stretches):
        wait_bytes(home.at[j - 1], back_z_recv.at[j])
    outs, row_grads = ([rows] for rows in unpaired(own_home[...]))
    for j in range(1, stretches):
        rows = home[j - 1].astype(F32)
        outs.append(rows[:room])
        row_grads.append(rows[room:])
    spare = slots - near_slots - (stretches - 1) * room
    if spare:
        outs.append(jnp.zeros((spare, lat), F32))
        row_grads.append(jnp.zeros((spare, lat), F32))
    out = jnp.concatenate(outs, axis=0)
    row_grad = jnp.concatenate(row_grads, axis=0)
    lat_ref[...] = dot(place_t[...], row_grad.astype(BF16)).astype(BF16)
    first, second, _ = parts_of(row_share[...] * out)
    comb_ref[...] = (dot(place_t[...], first) + dot(place_t[...], second)).astype(BF16)
    row_prob = jnp.sum(cot_rows[...].astype(F32) * out, axis=1, keepdims=True)
    by_expert = sum(
        dot_tn(part, place[...]) for part in parts_of(jnp.where(slot_expert, row_prob, 0.0))
    )
    for k in range(top):
        hit = picks[k : k + 1] == expert_row
        prob_ref[k : k + 1] = jnp.sum(jnp.where(hit, by_expert, 0.0), axis=0, keepdims=True)

    for copy in z_copies:
        copy.wait_send()
    wait_bytes(blocks_in, ag_x_send)
    wait_bytes(outbox, out_z_send)
    wait_bytes(inbox.at[:, pl.ds(1, members - 1)], out_y_send)
    wait_bytes(inbox.at[:, pl.ds(1, members - 1)], back_y_send)
    wait_bytes(home, back_z_send)
    for q in range(len(chunks)):
        wait_bytes(x_in.at[q], rs_x_send.at[q])
        wait_bytes(z_in.at[q], rs_z_send.at[q])


def layer(
    room,
    kernel_id,
    compressed_tokens,
    picked_specialists,
    gating_shares,
    seat_limits,
    raising_factors,
    lowering_factors,
    result_cotangent,
):
    runs, wide = DP_GRID
    ys, stretches, cores = EXPERT_GRID
    experts = ys * stretches * cores
    members = ys * cores
    tokens, lat = compressed_tokens.shape
    top = picked_specialists.shape[0]
    _, depth, hid = raising_factors.shape
    near_slots = members * SEATS
    slots = -(-(near_slots + (stretches - 1) * room) // 128) * 128
    rows = experts * SEATS
    vmem = pl.BlockSpec(memory_space=pltpu.VMEM)
    hbm = pl.BlockSpec(memory_space=pltpu.HBM)
    dma = pltpu.SemaphoreType.DMA
    blocks = pltpu.VMEM((stretches, members, PAIR, lat), BF16)
    far_blocks = pltpu.VMEM((stretches - 1, members, PAIR, lat), BF16)
    own_blocks = pltpu.VMEM((members, PAIR, lat), BF16)
    folded = pltpu.VMEM((stretches - 1, 2 * room, lat), BF16)
    outs = (
        jax.ShapeDtypeStruct((tokens, lat), BF16),
        jax.ShapeDtypeStruct((tokens, lat), BF16),
        jax.ShapeDtypeStruct((top, tokens), F32),
        jax.ShapeDtypeStruct((1, depth, hid), F32),
        jax.ShapeDtypeStruct((1, depth, hid), F32),
    )
    return pl.pallas_call(
        functools.partial(kernel, room),
        out_shape=outs,
        in_specs=[hbm] * 7,
        out_specs=[vmem] * 5,
        scratch_shapes=[
            pltpu.VMEM((2, runs, wide, depth, hid), BF16),
            pltpu.VMEM((tokens, lat), BF16),
            pltpu.VMEM((tokens, lat), BF16),
            pltpu.VMEM((top, tokens), jnp.int32),
            pltpu.VMEM((top, tokens), F32),
            pltpu.VMEM((1, experts), jnp.int32),
            own_blocks,
            folded,
            folded,
            blocks,
            blocks,
            far_blocks,
            folded,
            own_blocks,
            folded,
            pltpu.VMEM((slots, tokens), BF16),
            pltpu.VMEM((tokens, slots), BF16),
            pltpu.VMEM((members * PAIR, 2 * room), BF16),
            far_blocks,
            pltpu.VMEM((slots, lat), BF16),
            pltpu.VMEM((slots, 1), F32),
            pltpu.VMEM((rows, lat), BF16),
            pltpu.VMEM((rows, lat), BF16),
            pltpu.VMEM((rows, hid), BF16),
            pltpu.VMEM((rows, hid), BF16),
            pltpu.VMEM((2 * CHUNKS, runs, wide, depth, hid // CHUNKS), BF16),
            pltpu.VMEM((2 * CHUNKS, wide - 1, runs, depth, hid // CHUNKS), BF16),
            pltpu.VMEM((2 * CHUNKS, runs, depth, hid // CHUNKS), BF16),
            pltpu.VMEM((2 * CHUNKS, runs - 1, depth, hid // CHUNKS), BF16),
            dma((7,)),
            dma((runs,)),
            dma((runs,)),
            dma,
            dma,
            dma,
            dma((stretches,)),
            dma,
            dma((stretches,)),
            dma((stretches,)),
            dma,
            dma((stretches,)),
            dma,
            dma((stretches,)),
            dma((stretches,)),
            dma((2 * CHUNKS,)),
            dma((2 * CHUNKS,)),
            dma((2 * CHUNKS,)),
            dma((2 * CHUNKS,)),
            pltpu.SemaphoreType.REGULAR((2,)),
        ],
        compiler_params=pltpu.CompilerParams(
            collective_id=kernel_id, has_side_effects=True, vmem_limit_bytes=60 * 1024 * 1024
        ),
        name="moe_layer",
    )(
        compressed_tokens,
        result_cotangent,
        raising_factors,
        lowering_factors,
        picked_specialists,
        gating_shares,
        seat_limits,
    )


def body(
    compressed_tokens,
    picked_specialists,
    gating_shares,
    seat_limits,
    raising_factors,
    lowering_factors,
    result_cotangent,
):
    ys, stretches, cores = EXPERT_GRID
    most = jnp.max(jnp.sum(seat_limits.reshape(ys, stretches, cores), axis=(0, 2)))
    choice = sum((most > room).astype(jnp.int32) for room in ROOMS[:-1])
    combined, latent_grad, prob_grad, up_grad, down_grad = lax.switch(
        choice,
        [functools.partial(layer, room, i) for i, room in enumerate(ROOMS)],
        compressed_tokens,
        picked_specialists.T,
        gating_shares.T,
        seat_limits.reshape(1, -1),
        raising_factors,
        lowering_factors,
        result_cotangent,
    )
    return combined, latent_grad, prob_grad.T, up_grad, down_grad


def solution(mesh):
    in_specs = (
        P(("dp", "expert"), None),
        P(("dp", "expert"), None),
        P(("dp", "expert"), None),
        P(),
        P("expert", "dp", None),
        P("expert", "dp", None),
        P(("dp", "expert"), None),
    )
    out_specs = (
        P(("dp", "expert"), None),
        P(("dp", "expert"), None),
        P(("dp", "expert"), None),
        P("expert", "dp", None),
        P("expert", "dp", None),
    )
    return jax.shard_map(body, mesh=mesh, in_specs=in_specs, out_specs=out_specs, check_vma=False)
```

time: 156 us -> 143 us (0.917)
  Pallas kernels: 146 us -> 136 us
  local copies, waits for them, and re-layouts: 7.7 us -> 4.08 us
    pallas_call x1, Pallas kernels: 146 us -> 136 us  [layer(): pl.pallas_call(functools.partial(kernel, room), out_shape=outs, in_specs=...]
    unnamed x16 -> x11, local copies, waits for them, and re-layouts: 7.03 us -> 3.97 us
where the time goes in v2:
time: 143 us
  Pallas kernels  136 us (95%)
  local copies, waits for them, and re-layouts  4.08 us (3%)
  between operations  1.98 us (1%)
    pallas_call x1, Pallas kernels, layer(): pl.pallas_call(functools.partial(kernel, room), out_shape=outs, in_specs=...  136 us
    unnamed x11, local copies, waits for them, and re-layouts  3.97 us

profile of v2, /device:TPU:1, one launch (start us, length us, event | category | flops | bytes accessed | tf_op | source)
XLA Modules:
  0.0 142.9 jit_solution(11899714112664437119)
XLA Ops:
  0.6 0.0 copy-start.2
  0.6 0.6 copy-done.2
  1.3 0.1 reshape.16
  1.4 0.0 copy-start.1
  1.4 0.1 reduce_sum.9
  1.5 0.0 copy-start
  1.5 0.6 reduce_max.9
  3.5 0.0 copy-done.1
  3.5 0.0 copy-done
  3.5 136.1 %conditional.1 = ((bf16[256,512]{1,0:T(8,128)(2,1)S(1)}, bf16[256,512]{1,0:T(8,128)(2,1)S(1)}, f32[8,256]{1,0:T(8,128)S(1)}, f32[1,32,1024]{2,1,0:T(8,128)S(1)}, f32[1,32,1024]{2,1,0:T(8,128)S(1)})) conditional(s32[]{:T(128)} %clamp.3, (bf16[256,512]{1,0:T(8,128)(2,1)}, bf16[256,512]{1,0:T(8,128)(2,1)}, ...), branch_computations={%region_2.0_spmd, %region_3.0_spmd, %region_4.0_spmd} | conditional | bytes 8 | solution.py:536
  3.5 135.9 %moe_layer.3 = (bf16[256,512]{1,0:T(8,128)(2,1)S(1)}, bf16[256,512]{1,0:T(8,128)(2,1)S(1)}, f32[8,256]{1,0:T(8,128)S(1)}, f32[1,32,1024]{2,1,0:T(8,128)S(1)}, f32[1,32,1024]{2,1,0:T(8,128)S(1)}) custom-call(bf16[256,512]{1,0:T(8,128)(2,1)} %get-tuple-element.42.tok_hbm, bf16[256,512]{1,0:T(8,128)(2,1)} %get-tuple-element.43.cot_hbm, ...), custom_call_target="tpu_custom_call" | custom-call | tf_op jit(solution)/shard_map/cond/branch_0_fun/moe_layer/pallas_call | solution.py:453
  139.6 0.7 copy.32
  140.3 0.7 copy.33
  141.0 0.6 copy.34
  141.6 0.7 copy.35
  142.3 0.7 copy.36
Async XLA Ops:
  0.6 0.7 copy-start.2
  1.4 2.1 %copy-start.1 = (f32[256,8]{0,1:T(8,128)S(1)}, f32[256,8]{0,1:T(8,128)}, u32[]{:S(2)}) copy-start(f32[256,8]{0,1:T(8,128)} %param.12) | copy-start | bytes 24580
  1.5 1.9 %copy-start = (s32[256,8]{0,1:T(8,128)S(1)}, s32[256,8]{0,1:T(8,128)}, u32[]{:S(2)}) copy-start(s32[256,8]{0,1:T(8,128)} %param.11) | copy-start | bytes 24580

commit v3 on v2

--- a/solution.py
+++ b/solution.py
@@ -64,7 +64,7 @@
     load_sem, ag_z_send, ag_z_recv, ag_x_send, ag_x_recv,
     out_z_send, out_z_recv, out_y_send, out_y_recv, out_self,
     back_y_send, back_y_recv, back_z_send, back_z_recv, back_self,
-    rs_x_send, rs_x_recv, rs_z_send, rs_z_recv, turn_sem,
+    rs_x_send, rs_x_recv, rs_z_send, rs_z_recv,
 ):
     runs, wide = DP_GRID
     ys, stretches, cores = EXPERT_GRID
@@ -199,19 +199,31 @@
     loads[1].wait()
     pl.semaphore_wait(barrier, len(peers) + members - 1)
 
-    z_copies = []
-    own = weights.at[:, run, across]
-    for j in range(1, runs):
-        copy = remote(own, own, ag_z_send.at[j], ag_z_recv.at[j], run_peer(j))
+    z_copies = [
+        [
+            remote(
+                weights.at[w, run, across], weights.at[w, run, across],
+                ag_z_send.at[w, j], ag_z_recv.at[w, j], run_peer(j),
+            )
+            for j in range(1, runs)
+        ]
+        for w in range(2)
+    ]
+
+    def fan_out(w, block):
+        for j in range(1, wide):
+            part = weights.at[w, block, across]
+            remote(part, part, ag_x_send.at[w], ag_x_recv.at[w], wide_peer(j)).start()
+
+    def pass_on(w):
+        for j in range(1, runs):
+            z_copies[w][j - 1].wait_recv()
+            fan_out(w, lax.rem(run + runs - j, runs))
+
+    for copy in z_copies[0]:
         copy.start()
-        z_copies.append(copy)
-
-    def fan_out(block):
-        for j in range(1, wide):
-            part = weights.at[:, block, across]
-            remote(part, part, ag_x_send, ag_x_recv, wide_peer(j)).start()
-
-    fan_out(run)
+    for w in range(2):
+        fan_out(w, run)
 
     loads[5].wait()
     loads[6].wait()
@@ -241,12 +253,6 @@
 
         lax.fori_loop(1, members, send, 0)
 
-    spread(own_out, 0)
-
-    for j in range(1, runs):
-        z_copies[j - 1].wait_recv()
-        fan_out(lax.rem(run + runs - j, runs))
-
     order = sorted(range(1, stretches), key=lambda j: min(j, stretches - j))
     near, far = order[:-1], order[-1]
 
@@ -255,19 +261,12 @@
             outbox.at[j - 1], middle.at[j - 1], out_z_send, out_z_recv.at[j], stretch_peer(j)
         ).start()
 
-    def tell_run(turn):
-        for j in range(1, runs):
-            pl.semaphore_signal(
-                turn_sem.at[turn], inc=1, device_id=run_peer(j), device_id_type=MESH
-            )
-
-    def wait_run(turn):
-        pl.semaphore_wait(turn_sem.at[turn], runs - 1)
-
-    tell_run(0)
-    wait_run(0)
     for j in near:
         set_out(j)
+    spread(own_out, 0)
+    pass_on(0)
+    for copy in z_copies[1]:
+        copy.start()
 
     def arrive(j):
         wait_bytes(middle.at[j - 1], out_z_recv.at[j])
@@ -295,6 +294,8 @@
         out = dot_nt(hs[rows], weights[1].reshape(lat, hid))
         row_grad = dot_nt(acts[rows], weights[0].reshape(lat, hid))
         reply[there] = paired(out, row_grad, members)
+
+    def send_back(there):
         target = own_home if there == 0 else gather.at[there - 1]
         pltpu.make_async_copy(reply.at[there, 0], target.at[0], back_self.at[there]).start()
 
@@ -324,22 +325,23 @@
 
     for j in near:
         arrive(j)
-    tell_run(1)
-    for j in near:
         forward(j)
-    wait_run(1)
+    pass_on(1)
     set_out(far)
     place_t[...] = place[...].T
-    blocks_in = weights.at[:, :, pl.ds(0, wide - 1)]
-    wait_bytes(blocks_in, ag_x_recv)
-    expert_step(0)
+    for w in range(2):
+        wait_bytes(weights.at[w, :, pl.ds(0, wide - 1)], ag_x_recv.at[w])
     for j in near:
         expert_step(stretches - j)
+        send_back(stretches - j)
+    expert_step(0)
     arrive(far)
     forward(far)
     for j in near:
         go_home(stretches - j)
     expert_step(stretches - far)
+    send_back(stretches - far)
+    send_back(0)
 
     chunk_columns = hid // CHUNKS
     chunks = [
@@ -358,6 +360,7 @@
                 partial.at[q, :, there], x_in.at[q, j - 1],
                 rs_x_send.at[q], rs_x_recv.at[q], wide_peer(j),
             ).start()
+    go_home(stretches - far)
     for q in range(len(chunks)):
         wait_bytes(x_in.at[q], rs_x_recv.at[q])
         total = partial[q, :, across].astype(F32)
@@ -369,8 +372,6 @@
                 z_out.at[q, lax.rem(run + j, runs)], z_in.at[q, j - 1],
                 rs_z_send.at[q], rs_z_recv.at[q], run_peer(j),
             ).start()
-        if q == 0:
-            go_home(stretches - far)
     for q, (grad_ref, _, _, start) in enumerate(chunks):
         wait_bytes(z_in.at[q], rs_z_recv.at[q])
         total = z_out[q, run].astype(F32)
@@ -403,9 +404,10 @@
         hit = picks[k : k + 1] == expert_row
         prob_ref[k : k + 1] = jnp.sum(jnp.where(hit, by_expert, 0.0), axis=0, keepdims=True)
 
-    for copy in z_copies:
-        copy.wait_send()
-    wait_bytes(blocks_in, ag_x_send)
+    for w in range(2):
+        for copy in z_copies[w]:
+            copy.wait_send()
+        wait_bytes(weights.at[w, :, pl.ds(0, wide - 1)], ag_x_send.at[w])
     wait_bytes(outbox, out_z_send)
     wait_bytes(inbox.at[:, pl.ds(1, members - 1)], out_y_send)
     wait_bytes(inbox.at[:, pl.ds(1, members - 1)], back_y_send)
@@ -486,10 +488,10 @@
             pltpu.VMEM((2 * CHUNKS, runs, depth, hid // CHUNKS), BF16),
             pltpu.VMEM((2 * CHUNKS, runs - 1, depth, hid // CHUNKS), BF16),
             dma((7,)),
-            dma((runs,)),
-            dma((runs,)),
-            dma,
-            dma,
+            dma((2, runs)),
+            dma((2, runs)),
+            dma((2,)),
+            dma((2,)),
             dma,
             dma((stretches,)),
             dma,
@@ -504,7 +506,6 @@
             dma((2 * CHUNKS,)),
             dma((2 * CHUNKS,)),
             dma((2 * CHUNKS,)),
-            pltpu.SemaphoreType.REGULAR((2,)),
         ],
         compiler_params=pltpu.CompilerParams(
             collective_id=kernel_id, has_side_effects=True, vmem_limit_bytes=60 * 1024 * 1024
@@ -519,6 +520,12 @@
         gating_shares,
         seat_limits,
     )
+
+
+def store_kernel(*refs):
+    count = len(refs) // 2
+    for src, dst in zip(refs[:count], refs[count:]):
+        dst[...] = src[...]
 
 
 def body(
@@ -544,6 +551,15 @@
         lowering_factors,
         result_cotangent,
     )
+    vmem = pl.BlockSpec(memory_space=pltpu.VMEM)
+    results = (combined, latent_grad, prob_grad, up_grad, down_grad)
+    combined, latent_grad, prob_grad, up_grad, down_grad = pl.pallas_call(
+        store_kernel,
+        out_shape=tuple(jax.ShapeDtypeStruct(r.shape, r.dtype) for r in results),
+        in_specs=[vmem] * 5,
+        out_specs=[vmem] * 5,
+        name="store_results",
+    )(*results)
     return combined, latent_grad, prob_grad.T, up_grad, down_grad
 
 

time: 143 us -> 137 us (0.958)
  Pallas kernels: 136 us -> 132 us
  local copies, waits for them, and re-layouts: 4.08 us -> 0.77 us
    pallas_call x1, Pallas kernels: 136 us -> 131 us  [layer(): pl.pallas_call(functools.partial(kernel, room), out_shape=outs, in_specs=...]
    unnamed x11 -> x6, local copies, waits for them, and re-layouts: 3.97 us -> 0.66 us
where the time goes in v3:
time: 137 us; the launch traced here: 136 us
  Pallas kernels  132 us (96%)
  between operations  1.98 us (1%)
    pallas_call x1, Pallas kernels, layer(): pl.pallas_call(functools.partial(kernel, room), out_shape=outs, in_specs=...  131 us

profile of v3, /device:TPU:1, one launch (start us, length us, event | category | flops | bytes accessed | tf_op | source)
XLA Modules:
  0.0 136.2 jit_solution(1931708707349173023)
XLA Ops:
  0.6 0.0 copy-start.2
  0.6 0.6 copy-done.2
  1.3 0.1 reshape.16
  1.4 0.0 copy-start.1
  1.4 0.1 reduce_sum.9
  1.5 0.0 copy-start
  1.5 0.6 reduce_max.9
  3.5 0.0 copy-done.1
  3.5 0.0 copy-done
  3.5 131.8 %conditional.1 = ((bf16[256,512]{1,0:T(8,128)(2,1)S(1)}, bf16[256,512]{1,0:T(8,128)(2,1)S(1)}, f32[8,256]{1,0:T(8,128)S(1)}, f32[1,32,1024]{2,1,0:T(8,128)S(1)}, f32[1,32,1024]{2,1,0:T(8,128)S(1)})) conditional(s32[]{:T(128)} %clamp.3, (bf16[256,512]{1,0:T(8,128)(2,1)}, bf16[256,512]{1,0:T(8,128)(2,1)}, ...), branch_computations={%region_2.0_spmd, %region_3.0_spmd, %region_4.0_spmd} | conditional | bytes 8 | solution.py:543
  3.8 131.1 %moe_layer.4 = (bf16[256,512]{1,0:T(8,128)(2,1)S(1)}, bf16[256,512]{1,0:T(8,128)(2,1)S(1)}, f32[8,256]{1,0:T(8,128)S(1)}, f32[1,32,1024]{2,1,0:T(8,128)S(1)}, f32[1,32,1024]{2,1,0:T(8,128)S(1)}) custom-call(bf16[256,512]{1,0:T(8,128)(2,1)} %get-tuple-element.49.tok_hbm, bf16[256,512]{1,0:T(8,128)(2,1)} %get-tuple-element.50.cot_hbm, ...), custom_call_target="tpu_custom_call" | custom-call | tf_op jit(solution)/shard_map/cond/branch_1_fun/moe_layer/pallas_call | solution.py:455
  135.3 0.9 store_results.1
Async XLA Ops:
  0.6 0.7 copy-start.2
  1.4 2.1 %copy-start.1 = (f32[256,8]{0,1:T(8,128)S(1)}, f32[256,8]{0,1:T(8,128)}, u32[]{:S(2)}) copy-start(f32[256,8]{0,1:T(8,128)} %param.12) | copy-start | bytes 24580
  1.5 1.9 %copy-start = (s32[256,8]{0,1:T(8,128)S(1)}, s32[256,8]{0,1:T(8,128)}, u32[]{:S(2)}) copy-start(s32[256,8]{0,1:T(8,128)} %param.11) | copy-start | bytes 24580
